TPU v7x, 128 devices: a whole 4x4x4 slice. The times are simulated.
128 devices in a mesh: row: 16 (over x, z), col: 8 (over y, core).
Axes of the slice: x: 4, y: 4, z: 4, core: 2. Of those that a mesh axis runs over, the one named last changes fastest.
Arguments:
- tmatrix: bfloat16 [10656, 10656], P('row', 'col'), may hold values from -0.0625 to 0.0625
- panel: bfloat16 [10656, 2048], P('col', 'row'), may hold values from -6 to 6
- contrast: float32 [3, 144, 288], replicated, may hold values from -1.5 to 1.5
Outputs:
- excitation: bfloat16 [10656, 2048], P('col', 'row')
All inputs are finite; a program needn't handle non-finite values.
Results may differ from a plain program's by a relative error of at most 0.006.
Values may be sent and summed in bfloat16 or wider, within the bound.
A program may use at most 128 MiB of HBM per device.

v0:
```python
import functools

import jax
import jax.numpy as jnp
import ml_dtypes
import numpy as np
from jax import lax
from jax.experimental import pallas as pl
from jax.experimental.pallas import tpu as pltpu
from jax.sharding import PartitionSpec as P

LDEG = 72
ITERS = 2
NT = 2 * LDEG
NP = 4 * LDEG
NQ = 2 * LDEG + 1
NX = 4
NZ = 4
NY = 4
ROWS = 16
COLS = 8
BLK = 666
HALF = 672
QUART = HALF // 2
LANES = 768
WIN = LANES // 128
TPAD = 256
QPAD = 160
PER = 16
MIB = 1024 * 1024
MESH = pl.DeviceIdType.MESH


def angular_tables(degree):
    lat_count = 2 * degree
    lon_count = 4 * degree
    freq_count = 2 * degree + 1
    colatitude = (np.arange(lat_count) + 0.5) * np.pi / lat_count
    cos_col = np.cos(colatitude)
    sin_col = np.sin(colatitude)
    legendre = np.zeros((freq_count, degree, lat_count))
    diagonal_term = np.full(lat_count, np.sqrt(0.5))
    for order_m in range(degree + 1):
        if order_m > 0:
            diagonal_term = (
                diagonal_term * np.sqrt((2.0 * order_m + 1.0) / (2.0 * order_m)) * sin_col
            )
        earlier = np.zeros(lat_count)
        latest = diagonal_term
        for degree_l in range(order_m, degree + 1):
            if degree_l == order_m:
                current = diagonal_term
            elif degree_l == order_m + 1:
                current = np.sqrt(2.0 * order_m + 3.0) * cos_col * diagonal_term
            else:
                factor_a = np.sqrt((4.0 * degree_l**2 - 1.0) / (degree_l**2 - order_m**2))
                factor_b = np.sqrt(
                    ((degree_l - 1.0) ** 2 - order_m**2) / (4.0 * (degree_l - 1.0) ** 2 - 1.0)
                )
                current = factor_a * (cos_col * latest - factor_b * earlier)
            if degree_l > order_m:
                earlier, latest = (latest, current)
            if degree_l >= 1:
                legendre[order_m, degree_l - 1] = current
                if order_m >= 1:
                    legendre[degree + order_m, degree_l - 1] = current
    longitude = 2.0 * np.pi * np.arange(lon_count) / lon_count
    fourier = np.zeros((freq_count, lon_count))
    fourier[0] = 1.0 / np.sqrt(2.0 * np.pi)
    for order_m in range(1, degree + 1):
        fourier[order_m] = np.cos(order_m * longitude) / np.sqrt(np.pi)
        fourier[degree + order_m] = np.sin(order_m * longitude) / np.sqrt(np.pi)
    weight = sin_col * (np.pi / lat_count) * (2.0 * np.pi / lon_count)
    return (legendre, fourier, weight)


def meetings():
    owner = []
    for q in range(NQ):
        m = q if q <= LDEG else q - LDEG
        owner += [(q, l) for l in range(max(m, 1), LDEG + 1)]
    found = []
    for block in range(ROWS // 2):
        for window in range(WIN):
            first = block * BLK + window * 128
            last = min(first + 128, (block + 1) * BLK)
            for q in sorted({owner[n][0] for n in range(first, last)}):
                rows = [(n - first, owner[n][1] - 1) for n in range(first, last) if owner[n][0] == q]
                found.append((block, window, q, rows))
    return found


def split(table):
    high = table.astype(np.float32).astype(ml_dtypes.bfloat16)
    low = (table - high.astype(np.float64)).astype(np.float32).astype(ml_dtypes.bfloat16)
    return np.stack([high, low])


@functools.lru_cache(None)
def tables():
    legendre, fourier, weight = angular_tables(LDEG)
    found = meetings()
    windows = np.zeros((len(found), 128, TPAD))
    for index, (block, window, q, rows) in enumerate(found):
        for place, level in rows:
            windows[index, place, :NT] = legendre[q, level]
    padded = np.zeros((QPAD, NP))
    padded[:NQ] = fourier
    return (
        [f[:3] for f in found],
        windows.astype(np.float32).astype(ml_dtypes.bfloat16),
        split(np.ascontiguousarray(padded.T)),
        split(padded),
        weight.astype(np.float32),
    )


def dot(a, b):
    return jnp.dot(a, b, preferred_element_type=jnp.float32)


def two(value):
    high = value.astype(jnp.bfloat16)
    return high, (value - high.astype(jnp.float32)).astype(jnp.bfloat16)


def legendre_in(found, coefficients, w_ref, lat):
    by_q = {}
    for index, (block, window, q) in enumerate(found):
        by_q.setdefault(q, []).append((index, block, window))
    for q in range(NQ):
        total = None
        for index, block, window in by_q[q]:
            term = dot(coefficients(block, window), w_ref[index])
            total = term if total is None else total + term
        for half in range(2):
            lat[half, q * 32 : (q + 1) * 32, :] = total[:, half * 128 : half * 128 + 128]


def columns(fs_ref, fa_ref, cw_ref, lat, spec):
    def synthesis(place):
        rows = pl.ds(place, QPAD, stride=32)
        high, low = two(jnp.concatenate([lat[0, rows, :], lat[1, rows, :]], axis=1))
        return dot(fs_ref[0], high) + dot(fs_ref[1], high) + dot(fs_ref[0], low)

    def analysis(place, value):
        high, low = two(value)
        value = dot(fa_ref[0], high) + dot(fa_ref[1], high) + dot(fa_ref[0], low)
        for half in range(2):
            spec[half, pl.ds(place, QPAD, stride=32), :] = value[:, half * 128 : half * 128 + 128]

    def column(k, carry):
        first = synthesis(k)
        second = synthesis(PER + k)
        analysis(k, cw_ref[0] * first + cw_ref[1] * second)
        analysis(PER + k, cw_ref[1] * first + cw_ref[2] * second)
        return carry

    lax.fori_loop(0, PER, column, 0, unroll=2)


def legendre_out(found, w_ref, spec, b_ref, done):
    by_window = {}
    for index, (block, window, q) in enumerate(found):
        by_window.setdefault((block, window), []).append((index, q))
    for (block, window), members in sorted(by_window.items()):
        total = None
        for index, q in members:
            rows = slice(q * 32, (q + 1) * 32)
            high, low = two(jnp.concatenate([spec[0, rows, :], spec[1, rows, :]], axis=1))
            term = lax.dot_general(
                jnp.concatenate([high, low], axis=0),
                w_ref[index],
                (((1,), (1,)), ((), ())),
                preferred_element_type=jnp.float32,
            )
            total = term if total is None else total + term
        value = (total[:32] + total[32:]).astype(jnp.bfloat16)
        lanes = slice(window * 128, (window + 1) * 128)
        b_ref[block, :, lanes] = value[:PER]
        b_ref[block + 8, :, lanes] = value[PER:]
        if window == WIN - 1 and block % 2 == 1:
            done(block // 2)
            done(block // 2 + 4)


STEP = {"x+": (1, 0), "x-": (-1, 0), "z+": (0, 1), "z-": (0, -1)}
ALL = (0, 2 * HALF)
A = (0, HALF)
B = (HALF, HALF)
A0, A1 = (0, QUART), (QUART, QUART)
B0, B1 = (HALF, QUART), (HALF + QUART, QUART)


def ring_plan():
    plan = []

    def send(part, rel, way):
        plan.append(("send", part, (rel[0] % NX, rel[1] % NZ), way))

    def recv(part, rel, way):
        plan.append(("recv", part, (rel[0] % NX, rel[1] % NZ), way))

    def use(*rels):
        for rel in rels:
            plan.append(("use", (rel[0] % NX, rel[1] % NZ)))

    own = (0, 0)
    for way in ("x+", "x-"):
        send(A, own, way)
    for way in ("z+", "z-"):
        send(B, own, way)
    for way in ("z+", "z-"):
        send(A, own, way)
    for way in ("x+", "x-"):
        send(B, own, way)
    use(own)
    for part, quart, rel, way in ((A, A0, (-1, 0), "x+"), (A, A1, (1, 0), "x-")):
        recv(part, rel, way)
        send(quart, rel, way)
        send(A, rel, "z+")
        send(A, rel, "z-")
    for part, quart, rel, way in ((B, B0, (0, -1), "z+"), (B, B1, (0, 1), "z-")):
        recv(part, rel, way)
        send(quart, rel, way)
        send(B, rel, "x+")
        send(B, rel, "x-")
    for quart, rel, way in ((A0, (0, -1), "z+"), (A1, (0, 1), "z-")):
        recv(A, rel, way)
        send(quart, rel, way)
    for quart, rel, way in ((B0, (-1, 0), "x+"), (B1, (1, 0), "x-")):
        recv(B, rel, way)
        send(quart, rel, way)
    use((-1, 0), (1, 0))
    recv(A0, (2, 0), "x+")
    recv(A1, (2, 0), "x-")
    send(A, (2, 0), "z+")
    send(A, (2, 0), "z-")
    recv(B0, (0, 2), "z+")
    recv(B1, (0, 2), "z-")
    send(B, (0, 2), "x+")
    send(B, (0, 2), "x-")
    use((0, -1), (0, 1))
    for x in (-1, 1):
        for quart, z, way in ((A0, -1, "z+"), (A1, 1, "z-")):
            recv(A, (x, z), way)
            send(quart, (x, z), way)
    for z in (-1, 1):
        for quart, x, way in ((B0, -1, "x+"), (B1, 1, "x-")):
            recv(B, (x, z), way)
            send(quart, (x, z), way)
    use((-1, -1), (-1, 1))
    recv(A0, (0, 2), "z+")
    recv(A1, (0, 2), "z-")
    recv(B0, (2, 0), "x+")
    recv(B1, (2, 0), "x-")
    for quart, z, way in ((A0, -1, "z+"), (A1, 1, "z-")):
        recv(A, (2, z), way)
        send(quart, (2, z), way)
    for quart, x, way in ((B0, -1, "x+"), (B1, 1, "x-")):
        recv(B, (x, 2), way)
        send(quart, (x, 2), way)
    use((1, -1), (1, 1), (0, 2), (2, 0))
    for x in (-1, 1):
        recv(A0, (x, 2), "z+")
        recv(A1, (x, 2), "z-")
        use((x, 2))
    for z in (-1, 1):
        recv(B0, (2, z), "x+")
        recv(B1, (2, z), "x-")
        use((2, z))
    recv(A0, (2, 2), "z+")
    recv(A1, (2, 2), "z-")
    recv(B0, (2, 2), "x+")
    recv(B1, (2, 2), "x-")
    use((2, 2))
    return plan


def greet(others):
    barrier = pltpu.get_barrier_semaphore()
    for other in others:
        pl.semaphore_signal(barrier, inc=1, device_id=other, device_id_type=MESH)
    pl.semaphore_wait(barrier, len(others))


def step_kernel(
    plan,
    found,
    t_ref,
    panel_ref,
    contrast_ref,
    weight_ref,
    w_hbm,
    fs_ref,
    fa_ref,
    out_ref,
    held,
    prod,
    mate_out,
    mate_in,
    sums,
    y_in,
    z_out,
    s_in,
    b_out,
    b_in,
    w_ref,
    cw_ref,
    lat,
    spec,
    w_sem,
    ring_send,
    ring_recv,
    mate_send,
    mate_recv,
    y_send,
    y_recv,
    z_send,
    z_recv,
    b_send,
    b_recv,
):
    row = lax.axis_index("row")
    col = lax.axis_index("col")
    x, z = row // NZ, row % NZ
    y, core = col // 2, col % 2
    f32, bf16 = jnp.float32, jnp.bfloat16

    def block_of(rel):
        return ((x + rel[0] + NX) % NX) * NZ + (z + rel[1] + NZ) % NZ

    table_copy = pltpu.make_async_copy(w_hbm, w_ref, w_sem)
    table_copy.start()
    held[0, row] = panel_ref[...]
    greet(
        [{"row": (row + k) % ROWS} for k in range(1, ROWS)]
        + [{"col": (col + k) % COLS} for k in range(1, COLS)]
    )
    mate = {"col": y * 2 + (1 - core)}
    y_peers = [{"col": ((y + k) % NY) * 2 + core} for k in range(1, NY)]

    slot = {}
    for event in plan:
        if event[0] == "send":
            slot[event[1:]] = len(slot)
    order = [event[1] for event in plan if event[0] == "use"]

    def ring_copy(it, part, rel, way, number):
        here = held.at[it, block_of(rel), pl.ds(part[0], part[1])]
        return pltpu.make_async_remote_copy(
            src_ref=here,
            dst_ref=here,
            send_sem=ring_send.at[number],
            recv_sem=ring_recv.at[it, number],
            device_id={"row": block_of(STEP[way])},
            device_id_type=MESH,
        )

    def mate_copy(it, s):
        return pltpu.make_async_remote_copy(
            src_ref=mate_out.at[s],
            dst_ref=mate_in.at[it, s],
            send_sem=mate_send.at[s],
            recv_sem=mate_recv.at[it, s],
            device_id=mate,
            device_id_type=MESH,
        )

    def y_copy(it, s, k):
        to = (y + k) % NY
        number = s * 3 + k - 1
        return pltpu.make_async_remote_copy(
            src_ref=sums.at[s, pl.ds(pl.multiple_of(to * PER, PER), PER)],
            dst_ref=y_in.at[it, s, k - 1],
            send_sem=y_send.at[number],
            recv_sem=y_recv.at[it, number],
            device_id=y_peers[k - 1],
            device_id_type=MESH,
        )

    def z_copy(it, s):
        return pltpu.make_async_remote_copy(
            src_ref=z_out.at[s],
            dst_ref=s_in.at[it, row],
            send_sem=z_send.at[s],
            recv_sem=z_recv.at[it, s],
            device_id={"row": block_of(order[s])},
            device_id_type=MESH,
        )

    def z_arrival(it, s):
        back = (-order[s][0], -order[s][1])
        return pltpu.make_async_remote_copy(
            src_ref=z_out.at[s],
            dst_ref=s_in.at[it, block_of(back)],
            send_sem=z_send.at[s],
            recv_sem=z_recv.at[it, s],
            device_id={"row": block_of(back)},
            device_id_type=MESH,
        )

    def b_copy(it, k):
        return pltpu.make_async_remote_copy(
            src_ref=b_out.at[pl.ds(2 * k, 2)],
            dst_ref=b_in.at[it, core * NY + y],
            send_sem=b_send.at[k],
            recv_sem=b_recv.at[it, col],
            device_id={"col": k},
            device_id_type=MESH,
        )

    def b_arrival(it, k):
        return pltpu.make_async_remote_copy(
            src_ref=b_out.at[pl.ds(2 * k, 2)],
            dst_ref=b_in.at[it, k % 2 * NY + k // 2],
            send_sem=b_send.at[k],
            recv_sem=b_recv.at[it, k],
            device_id={"col": k},
            device_id_type=MESH,
        )

    def multiply(it, s, rel):
        block = block_of(rel)
        here = s % 4
        for chunk in range(LANES // 256):
            rows = slice(chunk * 256, (chunk + 1) * 256)
            value = dot(t_ref[0, rows], held[it, block, 0:HALF])
            value += dot(t_ref[1, rows], held[it, block, HALF : 2 * HALF])
            prod[here, :, rows] = value.T
        start = pl.multiple_of((1 - core) * 64, 64)
        mate_out[s] = prod[here, pl.ds(start, 64), :].astype(bf16)
        mate_copy(it, s).start()

    def add_mate(it, s):
        mate_copy(it, s).wait_recv()
        start = pl.multiple_of(core * 64, 64)
        sums[s] = (prod[s % 4, pl.ds(start, 64), :] + mate_in[it, s].astype(f32)).astype(bf16)
        for k in (2, 1, 3):
            y_copy(it, s, k).start()

    def add_y(it, s):
        total = sums[s, pl.ds(pl.multiple_of(y * PER, PER), PER)].astype(f32)
        for k in range(1, NY):
            y_copy(it, s, k).wait_recv()
            total += y_in[it, s, k - 1].astype(f32)
        if s == 0:
            s_in[it, row] = total.astype(bf16)
        else:
            z_out[s] = total.astype(bf16)
            z_copy(it, s).start()

    def prepare():
        for part in range(3):
            turned = contrast_ref[part].T * weight_ref[:, :NT]
            cw_ref[part] = jnp.concatenate([turned, jnp.zeros((NP, TPAD - NT), f32)], axis=1)
        lat[:, NQ * 32 :, :] = jnp.zeros((2, QPAD * 32 - NQ * 32, 128), f32)

    def iteration(it, carry):
        s = 0
        for event in plan:
            if event[0] == "send":
                _, part, rel, way = event
                ring_copy(it, part, rel, way, slot[event[1:]]).start()
            elif event[0] == "recv":
                _, part, rel, way = event
                there = ((rel[0] + STEP[way][0]) % NX, (rel[1] + STEP[way][1]) % NZ)
                ring_copy(it, part, rel, way, slot[(part, there, way)]).wait_recv()
            else:
                multiply(it, s, event[1])
                if s == 0:
                    pl.when(it == 0)(prepare)
                if s >= 3:
                    add_mate(it, s - 3)
                if s >= 7:
                    add_y(it, s - 7)
                s += 1
        for late in range(ROWS, ROWS + 3):
            add_mate(it, late - 3)
            add_y(it, late - 7)
        for late in range(ROWS - 4, ROWS):
            add_y(it, late)
        pl.when(it == 0)(table_copy.wait)
        for s in range(1, ROWS):
            z_arrival(it, s).wait_recv()

        def coefficients(block, window):
            lanes = slice(window * 128, (window + 1) * 128)
            return jnp.concatenate([s_in[it, block, :, lanes], s_in[it, block + 8, :, lanes]], axis=0)

        legendre_in(found, coefficients, w_ref, lat)
        columns(fs_ref, fa_ref, cw_ref, lat, spec)

        def done(k):
            @pl.when(col != k)
            def _():
                b_copy(it, k).start()

        legendre_out(found, w_ref, spec, b_out, done)
        b_in[it, core * NY + y] = b_out[pl.ds(2 * col, 2)]
        for event in plan:
            if event[0] == "send":
                _, part, rel, way = event
                ring_copy(it, part, rel, way, slot[event[1:]]).wait_send()
        for s in range(ROWS):
            mate_copy(it, s).wait_send()
            for k in range(1, NY):
                y_copy(it, s, k).wait_send()
            if s > 0:
                z_copy(it, s).wait_send()
        for k in range(COLS):

            @pl.when(col != k)
            def _():
                b_arrival(it, k).wait_recv()

        for half in range(2):
            rows = slice(half * HALF, (half + 1) * HALF)
            value = jnp.concatenate([b_in[it, k, half].astype(f32) for k in range(COLS)], axis=0)
            value = (value.T[:HALF] + panel_ref[rows].astype(f32)).astype(bf16)

            @pl.when(it == 0)
            def _():
                held[1, row, rows] = value

            @pl.when(it == 1)
            def _():
                out_ref[rows] = value

        for k in range(COLS):

            @pl.when(col != k)
            def _():
                b_copy(it, k).wait_send()

        return carry

    lax.fori_loop(0, ITERS, iteration, 0)


def steps(t, panel, contrast, weight, w, fs, fa, found):
    plan = ring_plan()
    sends = sum(event[0] == "send" for event in plan)
    vmem = pl.BlockSpec(memory_space=pltpu.VMEM)
    dma = pltpu.SemaphoreType.DMA
    bf16, f32 = jnp.bfloat16, jnp.float32
    return pl.pallas_call(
        functools.partial(step_kernel, plan, found),
        out_shape=jax.ShapeDtypeStruct((2 * HALF, 128), bf16),
        in_specs=[vmem] * 4 + [pl.BlockSpec(memory_space=pl.ANY)] + [vmem] * 2,
        out_specs=vmem,
        scratch_shapes=[
            pltpu.VMEM((ITERS, ROWS, 2 * HALF, 128), bf16),
            pltpu.VMEM((4, 128, LANES), f32),
            pltpu.VMEM((ROWS, 64, LANES), bf16),
            pltpu.VMEM((ITERS, ROWS, 64, LANES), bf16),
            pltpu.VMEM((ROWS, 64, LANES), bf16),
            pltpu.VMEM((ITERS, ROWS, NY - 1, PER, LANES), bf16),
            pltpu.VMEM((ROWS, PER, LANES), bf16),
            pltpu.VMEM((ITERS, ROWS, PER, LANES), bf16),
            pltpu.VMEM((ROWS, PER, LANES), bf16),
            pltpu.VMEM((ITERS, COLS, 2, PER, LANES), bf16),
            pltpu.VMEM(w.shape, bf16),
            pltpu.VMEM((3, NP, TPAD), f32),
            pltpu.VMEM((2, QPAD * 32, 128), f32),
            pltpu.VMEM((2, QPAD * 32, 128), f32),
            dma(()),
            dma((sends,)),
            dma((ITERS, sends)),
            dma((ROWS,)),
            dma((ITERS, ROWS)),
            dma((ROWS * 3,)),
            dma((ITERS, ROWS * 3)),
            dma((ROWS,)),
            dma((ITERS, ROWS)),
            dma((COLS,)),
            dma((ITERS, COLS)),
        ],
        compiler_params=pltpu.CompilerParams(
            collective_id=0, has_side_effects=True, vmem_limit_bytes=58 * MIB
        ),
        name="steps",
    )(t, panel, contrast, weight, w, fs, fa)


def body(tmatrix, panel, contrast):
    found, windows, fs, fa, weight = tables()
    t = jnp.stack([tmatrix[:, :BLK], tmatrix[:, BLK:]])
    t = jnp.pad(t, ((0, 0), (0, LANES - BLK), (0, HALF - BLK)))
    pad = jnp.pad(panel.reshape(2, BLK, 128), ((0, 0), (0, HALF - BLK), (0, 0)))
    weight = jnp.asarray(np.pad(weight, (0, TPAD - NT)).reshape(1, TPAD))
    u = steps(
        t,
        pad.reshape(2 * HALF, 128),
        contrast,
        weight,
        jnp.asarray(windows),
        jnp.asarray(fs),
        jnp.asarray(fa),
        found,
    )
    return jnp.concatenate([u[:BLK], u[HALF : HALF + BLK]], axis=0)


def solution(mesh):
    placed = (P("row", "col"), P("col", "row"), P())
    return jax.shard_map(
        body, mesh=mesh, in_specs=placed, out_specs=P("col", "row"), check_vma=False
    )
```

profile of v0, /device:TPU:25, one launch (start us, length us, event | category | flops | bytes accessed | tf_op | source)
XLA Modules:
  0.0 165.5 jit_solution(13643284366186290940)
XLA Ops:
  0.0 2.1 %slice_bitcast_fusion.1 = (bf16[1,666,666]{2,1,0:T(8,128)(2,1)S(1)}, bf16[1,666,666]{2,1,0:T(8,128)(2,1)S(1)}) fusion(bf16[666,1332]{1,0:T(8,128)(2,1)} %param.7), kind=kLoop, calls=%fused_computation.9 | loop fusion | bytes 3548448 | tf_op jit(solution)/shard_map/stack | solution.py:588
  2.1 0.0 copy-start
  2.1 1.7 %fusion.5.t_ref = bf16[2,768,672]{2,1,0:T(8,128)(2,1)} fusion(bf16[1,666,666]{2,1,0:T(8,128)(2,1)S(1)} %get-tuple-element.6, bf16[1,666,666]{2,1,0:T(8,128)(2,1)S(1)} %get-tuple-element.5), kind=kLoop, calls=%fused_computation.7 | loop fusion | flops 11354112 | bytes 3838608 | tf_op jit(solution)/shard_map/stack | solution.py:588
  3.8 0.0 copy-done
  3.8 0.1 reshape.6
  3.9 0.8 pad.9
  4.6 159.0 %steps.1 = bf16[1344,128]{1,0:T(8,128)(2,1)} custom-call(bf16[2,768,672]{2,1,0:T(8,128)(2,1)} %fusion.5.t_ref, bf16[1344,128]{1,0:T(8,128)(2,1)} %bitcast.5, f32[3,144,288]{2,1,0:T(8,128)} %contrast_ref.1, f32[1,256]{1,0:T(1,128)} %constant.11.clone.weight_ref, bf16[188,128,256]{2,1,0:T(8,128)(2,1)} %constant.12.clone.w_hbm, ...), custom_call_target="tpu_custom_call" | custom-call | tf_op jit(solution)/shard_map/steps/pallas_call | solution.py:547
  163.7 1.0 fusion.6
  164.7 0.8 pad_maximum_fusion
Async XLA Ops:
  2.1 1.7 %copy-start = (bf16[1332,128]{1,0:T(8,128)(2,1)S(1)}, bf16[1332,128]{1,0:T(8,128)(2,1)}, u32[]{:S(2)}) copy-start(bf16[1332,128]{1,0:T(8,128)(2,1)} %param.8) | copy-start | bytes 1022980
where the time goes:
time: 166 us
  Pallas kernels  159 us (96%)
  local copies, waits for them, and re-layouts  3.98 us (2%)
  other arithmetic  2.46 us (1%)
    pallas_call x1, Pallas kernels, steps(): pl.pallas_call(functools.partial(step_kernel, plan, found), out_shape=jax...  159 us

commit v1 on v0

--- a/solution.py
+++ b/solution.py
@@ -21,12 +21,14 @@
 COLS = 8
 BLK = 666
 HALF = 672
-QUART = HALF // 2
 LANES = 768
 WIN = LANES // 128
 TPAD = 256
 QPAD = 160
-PER = 16
+PHASES = 2 * ITERS
+PER = 8
+CC = 2 * PER
+STEPS = ROWS // 2
 MIB = 1024 * 1024
 MESH = pl.DeviceIdType.MESH
 
@@ -134,12 +136,12 @@
             term = dot(coefficients(block, window), w_ref[index])
             total = term if total is None else total + term
         for half in range(2):
-            lat[half, q * 32 : (q + 1) * 32, :] = total[:, half * 128 : half * 128 + 128]
-
-
-def columns(fs_ref, fa_ref, cw_ref, lat, spec):
+            lat[half, q * CC : (q + 1) * CC, :] = total[:, half * 128 : half * 128 + 128]
+
+
+def columns(some, fs_ref, fa_ref, cw_ref, lat, spec):
     def synthesis(place):
-        rows = pl.ds(place, QPAD, stride=32)
+        rows = pl.ds(place, QPAD, stride=CC)
         high, low = two(jnp.concatenate([lat[0, rows, :], lat[1, rows, :]], axis=1))
         return dot(fs_ref[0], high) + dot(fs_ref[1], high) + dot(fs_ref[0], low)
 
@@ -147,49 +149,43 @@
         high, low = two(value)
         value = dot(fa_ref[0], high) + dot(fa_ref[1], high) + dot(fa_ref[0], low)
         for half in range(2):
-            spec[half, pl.ds(place, QPAD, stride=32), :] = value[:, half * 128 : half * 128 + 128]
-
-    def column(k, carry):
+            spec[half, pl.ds(place, QPAD, stride=CC), :] = value[:, half * 128 : half * 128 + 128]
+
+    for k in some:
         first = synthesis(k)
         second = synthesis(PER + k)
         analysis(k, cw_ref[0] * first + cw_ref[1] * second)
         analysis(PER + k, cw_ref[1] * first + cw_ref[2] * second)
-        return carry
-
-    lax.fori_loop(0, PER, column, 0, unroll=2)
-
-
-def legendre_out(found, w_ref, spec, b_ref, done):
+
+
+def legendre_out(found, pair, w_ref, spec, b_ref):
     by_window = {}
     for index, (block, window, q) in enumerate(found):
         by_window.setdefault((block, window), []).append((index, q))
-    for (block, window), members in sorted(by_window.items()):
-        total = None
-        for index, q in members:
-            rows = slice(q * 32, (q + 1) * 32)
-            high, low = two(jnp.concatenate([spec[0, rows, :], spec[1, rows, :]], axis=1))
-            term = lax.dot_general(
-                jnp.concatenate([high, low], axis=0),
-                w_ref[index],
-                (((1,), (1,)), ((), ())),
-                preferred_element_type=jnp.float32,
-            )
-            total = term if total is None else total + term
-        value = (total[:32] + total[32:]).astype(jnp.bfloat16)
+    for window in range(WIN):
+        values = []
+        for block in (2 * pair, 2 * pair + 1):
+            total = None
+            for index, q in by_window[block, window]:
+                rows = slice(q * CC, (q + 1) * CC)
+                high, low = two(jnp.concatenate([spec[0, rows, :], spec[1, rows, :]], axis=1))
+                term = lax.dot_general(
+                    jnp.concatenate([high, low], axis=0),
+                    w_ref[index],
+                    (((1,), (1,)), ((), ())),
+                    preferred_element_type=jnp.float32,
+                )
+                total = term if total is None else total + term
+            values.append(total[:CC] + total[CC:])
         lanes = slice(window * 128, (window + 1) * 128)
-        b_ref[block, :, lanes] = value[:PER]
-        b_ref[block + 8, :, lanes] = value[PER:]
-        if window == WIN - 1 and block % 2 == 1:
-            done(block // 2)
-            done(block // 2 + 4)
+        for c in range(2):
+            part = [value[c * PER : (c + 1) * PER] for value in values]
+            b_ref[pair + 4 * c, :, lanes] = jnp.concatenate(part, axis=0).astype(jnp.bfloat16)
 
 
 STEP = {"x+": (1, 0), "x-": (-1, 0), "z+": (0, 1), "z-": (0, -1)}
-ALL = (0, 2 * HALF)
-A = (0, HALF)
-B = (HALF, HALF)
-A0, A1 = (0, QUART), (QUART, QUART)
-B0, B1 = (HALF, QUART), (HALF + QUART, QUART)
+A, A0, A1 = (0, 336), (0, 176), (176, 160)
+B, B0, B1 = (336, 336), (336, 176), (512, 160)
 
 
 def ring_plan():
@@ -332,7 +328,8 @@
 
     table_copy = pltpu.make_async_copy(w_hbm, w_ref, w_sem)
     table_copy.start()
-    held[0, row] = panel_ref[...]
+    for phase in range(2):
+        held[phase, row] = panel_ref[phase]
     greet(
         [{"row": (row + k) % ROWS} for k in range(1, ROWS)]
         + [{"col": (col + k) % COLS} for k in range(1, COLS)]
@@ -351,7 +348,7 @@
         return pltpu.make_async_remote_copy(
             src_ref=here,
             dst_ref=here,
-            send_sem=ring_send.at[number],
+            send_sem=ring_send.at[it % 2, number],
             recv_sem=ring_recv.at[it, number],
             device_id={"row": block_of(STEP[way])},
             device_id_type=MESH,
@@ -371,7 +368,7 @@
         to = (y + k) % NY
         number = s * 3 + k - 1
         return pltpu.make_async_remote_copy(
-            src_ref=sums.at[s, pl.ds(pl.multiple_of(to * PER, PER), PER)],
+            src_ref=sums.at[s, pl.ds(pl.multiple_of(to * CC, CC), CC)],
             dst_ref=y_in.at[it, s, k - 1],
             send_sem=y_send.at[number],
             recv_sem=y_recv.at[it, number],
@@ -402,7 +399,7 @@
 
     def b_copy(it, k):
         return pltpu.make_async_remote_copy(
-            src_ref=b_out.at[pl.ds(2 * k, 2)],
+            src_ref=b_out.at[k],
             dst_ref=b_in.at[it, core * NY + y],
             send_sem=b_send.at[k],
             recv_sem=b_recv.at[it, col],
@@ -412,7 +409,7 @@
 
     def b_arrival(it, k):
         return pltpu.make_async_remote_copy(
-            src_ref=b_out.at[pl.ds(2 * k, 2)],
+            src_ref=b_out.at[k],
             dst_ref=b_in.at[it, k % 2 * NY + k // 2],
             send_sem=b_send.at[k],
             recv_sem=b_recv.at[it, k],
@@ -420,122 +417,181 @@
             device_id_type=MESH,
         )
 
-    def multiply(it, s, rel):
-        block = block_of(rel)
-        here = s % 4
+    def multiply(it, s):
+        first, second = [block_of(rel) for rel in order[2 * s : 2 * s + 2]]
+        here = s % 2
+        one, other = held[it, first], held[it, second]
+        lower = jnp.concatenate([one[:, :64], other[:, :64]], axis=1)
+        upper = jnp.concatenate([one[:, 64:], other[:, 64:]], axis=1)
         for chunk in range(LANES // 256):
             rows = slice(chunk * 256, (chunk + 1) * 256)
-            value = dot(t_ref[0, rows], held[it, block, 0:HALF])
-            value += dot(t_ref[1, rows], held[it, block, HALF : 2 * HALF])
-            prod[here, :, rows] = value.T
-        start = pl.multiple_of((1 - core) * 64, 64)
-        mate_out[s] = prod[here, pl.ds(start, 64), :].astype(bf16)
+            prod[here, :, rows] = (dot(t_ref[0, rows], lower) + dot(t_ref[1, rows], upper)).T
+        mate_out[s] = core_rows(here, 1 - core).astype(bf16)
         mate_copy(it, s).start()
+
+    def core_rows(here, which):
+        start = pl.multiple_of(which * 32, 32)
+        return jnp.concatenate([prod[here, pl.ds(start, 32), :], prod[here, pl.ds(64 + start, 32), :]], axis=0)
 
     def add_mate(it, s):
         mate_copy(it, s).wait_recv()
-        start = pl.multiple_of(core * 64, 64)
-        sums[s] = (prod[s % 4, pl.ds(start, 64), :] + mate_in[it, s].astype(f32)).astype(bf16)
+        value = core_rows(s % 2, core) + mate_in[it, s].astype(f32)
+        for owner in range(NY):
+            part = [value[k * 32 + owner * PER : k * 32 + (owner + 1) * PER] for k in range(2)]
+            sums[s, owner * CC : (owner + 1) * CC, :] = jnp.concatenate(part, axis=0).astype(bf16)
         for k in (2, 1, 3):
             y_copy(it, s, k).start()
 
     def add_y(it, s):
-        total = sums[s, pl.ds(pl.multiple_of(y * PER, PER), PER)].astype(f32)
+        total = sums[s, pl.ds(pl.multiple_of(y * CC, CC), CC)].astype(f32)
         for k in range(1, NY):
             y_copy(it, s, k).wait_recv()
             total += y_in[it, s, k - 1].astype(f32)
-        if s == 0:
-            s_in[it, row] = total.astype(bf16)
-        else:
-            z_out[s] = total.astype(bf16)
-            z_copy(it, s).start()
+        for k in range(2):
+            part = total[k * PER : (k + 1) * PER]
+            folded = jnp.concatenate([part[:, : LANES // 2], part[:, LANES // 2 :]], axis=0).astype(bf16)
+            if s == 0 and k == 0:
+                s_in[it, row] = folded
+            else:
+                z_out[2 * s + k] = folded
+                z_copy(it, 2 * s + k).start()
 
     def prepare():
         for part in range(3):
             turned = contrast_ref[part].T * weight_ref[:, :NT]
             cw_ref[part] = jnp.concatenate([turned, jnp.zeros((NP, TPAD - NT), f32)], axis=1)
-        lat[:, NQ * 32 :, :] = jnp.zeros((2, QPAD * 32 - NQ * 32, 128), f32)
-
-    def iteration(it, carry):
-        s = 0
+        lat[:, NQ * CC :, :] = jnp.zeros((2, (QPAD - NQ) * CC, 128), f32)
+
+    def own_sends(it):
         for event in plan:
-            if event[0] == "send":
+            if event[0] == "send" and event[2] == (0, 0):
                 _, part, rel, way = event
                 ring_copy(it, part, rel, way, slot[event[1:]]).start()
-            elif event[0] == "recv":
-                _, part, rel, way = event
-                there = ((rel[0] + STEP[way][0]) % NX, (rel[1] + STEP[way][1]) % NZ)
-                ring_copy(it, part, rel, way, slot[(part, there, way)]).wait_recv()
-            else:
-                multiply(it, s, event[1])
-                if s == 0:
-                    pl.when(it == 0)(prepare)
-                if s >= 3:
-                    add_mate(it, s - 3)
-                if s >= 7:
-                    add_y(it, s - 7)
-                s += 1
-        for late in range(ROWS, ROWS + 3):
-            add_mate(it, late - 3)
-            add_y(it, late - 7)
-        for late in range(ROWS - 4, ROWS):
-            add_y(it, late)
-        pl.when(it == 0)(table_copy.wait)
-        for s in range(1, ROWS):
-            z_arrival(it, s).wait_recv()
-
-        def coefficients(block, window):
-            lanes = slice(window * 128, (window + 1) * 128)
-            return jnp.concatenate([s_in[it, block, :, lanes], s_in[it, block + 8, :, lanes]], axis=0)
-
-        legendre_in(found, coefficients, w_ref, lat)
-        columns(fs_ref, fa_ref, cw_ref, lat, spec)
-
-        def done(k):
-            @pl.when(col != k)
-            def _():
-                b_copy(it, k).start()
-
-        legendre_out(found, w_ref, spec, b_out, done)
-        b_in[it, core * NY + y] = b_out[pl.ds(2 * col, 2)]
+
+    def gathering(it):
+        groups, events, uses = [], [], 0
+        for event in plan:
+            if event[0] == "use":
+                uses += 1
+                if uses % 2 == 0:
+                    groups.append(events)
+                    events = []
+            elif event[0] == "recv" or event[2] != (0, 0):
+                events.append(event)
+
+        def ticks(s):
+            if s < STEPS:
+                for kind, part, rel, way in groups[s]:
+                    if kind == "send":
+                        ring_copy(it, part, rel, way, slot[(part, rel, way)]).start()
+                    else:
+                        there = ((rel[0] + STEP[way][0]) % NX, (rel[1] + STEP[way][1]) % NZ)
+                        ring_copy(it, part, rel, way, slot[(part, there, way)]).wait_recv()
+                multiply(it, s)
+            if 0 <= s - 1 < STEPS:
+                add_mate(it, s - 1)
+            if 0 <= s - 3 < STEPS:
+                add_y(it, s - 3)
+
+        return [functools.partial(ticks, s) for s in range(STEPS + 3)]
+
+    def sent(it):
         for event in plan:
             if event[0] == "send":
                 _, part, rel, way = event
                 ring_copy(it, part, rel, way, slot[event[1:]]).wait_send()
-        for s in range(ROWS):
+        for s in range(STEPS):
             mate_copy(it, s).wait_send()
             for k in range(1, NY):
                 y_copy(it, s, k).wait_send()
-            if s > 0:
-                z_copy(it, s).wait_send()
+        for s in range(1, ROWS):
+            z_copy(it, s).wait_send()
+
+    def couple(it, ticks):
+        ticks = list(ticks)
+
+        def tick(count):
+            for _ in range(count):
+                if ticks:
+                    ticks.pop(0)()
+
+        for s in range(1, ROWS):
+            z_arrival(it, s).wait_recv()
+
+        def coefficients(block, window):
+            low = window % 3 * 128
+            lanes = slice(low, low + 128)
+            rows = slice(window // 3 * PER, (window // 3 + 1) * PER)
+            both = [s_in[it, b, :, lanes].astype(f32)[rows] for b in (block, block + 8)]
+            return jnp.concatenate(both, axis=0).astype(bf16)
+
+        tick(1)
+        legendre_in(found, coefficients, w_ref, lat)
+        tick(1)
+        for k in range(0, PER, 2):
+            columns((k, k + 1), fs_ref, fa_ref, cw_ref, lat, spec)
+            tick(2)
+        for pair in range(4):
+            legendre_out(found, pair, w_ref, spec, b_out)
+            for k in (pair, pair + 4):
+
+                @pl.when(col != k)
+                def _():
+                    b_copy(it, k).start()
+
+            tick(1)
+        b_in[it, core * NY + y] = b_out[col]
+        tick(len(ticks))
+
+    def come_back(it):
         for k in range(COLS):
 
             @pl.when(col != k)
             def _():
                 b_arrival(it, k).wait_recv()
 
-        for half in range(2):
-            rows = slice(half * HALF, (half + 1) * HALF)
-            value = jnp.concatenate([b_in[it, k, half].astype(f32) for k in range(COLS)], axis=0)
-            value = (value.T[:HALF] + panel_ref[rows].astype(f32)).astype(bf16)
-
-            @pl.when(it == 0)
-            def _():
-                held[1, row, rows] = value
-
-            @pl.when(it == 1)
-            def _():
-                out_ref[rows] = value
-
+        came = [b_in[it, k].astype(f32) for k in range(COLS)]
+        value = jnp.concatenate([c[:PER] for c in came] + [c[PER:] for c in came], axis=0)
+        return (value.T[:HALF] + panel_ref[it % 2].astype(f32)).astype(bf16)
+
+    def returned(it):
         for k in range(COLS):
 
             @pl.when(col != k)
             def _():
                 b_copy(it, k).wait_send()
 
+    own_sends(0)
+    for s, tick in enumerate(gathering(0)):
+        tick()
+        if s == 0:
+            prepare()
+        if s == STEPS - 1:
+            own_sends(1)
+    sent(0)
+    table_copy.wait()
+
+    def phase(it, carry):
+        couple(it, gathering(it + 1))
+        value = come_back(it)
+
+        @pl.when(it < PHASES - 2)
+        def _():
+            held[it + 2, row] = value
+            own_sends(it + 2)
+
+        @pl.when(it == PHASES - 2)
+        def _():
+            out_ref[0] = value
+
+        returned(it)
+        sent(it + 1)
         return carry
 
-    lax.fori_loop(0, ITERS, iteration, 0)
+    lax.fori_loop(0, PHASES - 1, phase, 0)
+    couple(PHASES - 1, [])
+    out_ref[1] = come_back(PHASES - 1)
+    returned(PHASES - 1)
 
 
 def steps(t, panel, contrast, weight, w, fs, fa, found):
@@ -546,35 +602,35 @@
     bf16, f32 = jnp.bfloat16, jnp.float32
     return pl.pallas_call(
         functools.partial(step_kernel, plan, found),
-        out_shape=jax.ShapeDtypeStruct((2 * HALF, 128), bf16),
+        out_shape=jax.ShapeDtypeStruct((2, HALF, 128), bf16),
         in_specs=[vmem] * 4 + [pl.BlockSpec(memory_space=pl.ANY)] + [vmem] * 2,
         out_specs=vmem,
         scratch_shapes=[
-            pltpu.VMEM((ITERS, ROWS, 2 * HALF, 128), bf16),
-            pltpu.VMEM((4, 128, LANES), f32),
-            pltpu.VMEM((ROWS, 64, LANES), bf16),
-            pltpu.VMEM((ITERS, ROWS, 64, LANES), bf16),
-            pltpu.VMEM((ROWS, 64, LANES), bf16),
-            pltpu.VMEM((ITERS, ROWS, NY - 1, PER, LANES), bf16),
-            pltpu.VMEM((ROWS, PER, LANES), bf16),
-            pltpu.VMEM((ITERS, ROWS, PER, LANES), bf16),
-            pltpu.VMEM((ROWS, PER, LANES), bf16),
-            pltpu.VMEM((ITERS, COLS, 2, PER, LANES), bf16),
+            pltpu.VMEM((PHASES, ROWS, HALF, 128), bf16),
+            pltpu.VMEM((2, 128, LANES), f32),
+            pltpu.VMEM((STEPS, 64, LANES), bf16),
+            pltpu.VMEM((PHASES, STEPS, 64, LANES), bf16),
+            pltpu.VMEM((STEPS, 64, LANES), bf16),
+            pltpu.VMEM((PHASES, STEPS, NY - 1, CC, LANES), bf16),
+            pltpu.VMEM((ROWS, CC, LANES // 2), bf16),
+            pltpu.VMEM((PHASES, ROWS, CC, LANES // 2), bf16),
+            pltpu.VMEM((COLS, CC, LANES), bf16),
+            pltpu.VMEM((PHASES, COLS, CC, LANES), bf16),
             pltpu.VMEM(w.shape, bf16),
             pltpu.VMEM((3, NP, TPAD), f32),
-            pltpu.VMEM((2, QPAD * 32, 128), f32),
-            pltpu.VMEM((2, QPAD * 32, 128), f32),
+            pltpu.VMEM((2, QPAD * CC, 128), f32),
+            pltpu.VMEM((2, QPAD * CC, 128), f32),
             dma(()),
-            dma((sends,)),
-            dma((ITERS, sends)),
+            dma((2, sends)),
+            dma((PHASES, sends)),
+            dma((STEPS,)),
+            dma((PHASES, STEPS)),
+            dma((STEPS * 3,)),
+            dma((PHASES, STEPS * 3)),
             dma((ROWS,)),
-            dma((ITERS, ROWS)),
-            dma((ROWS * 3,)),
-            dma((ITERS, ROWS * 3)),
-            dma((ROWS,)),
-            dma((ITERS, ROWS)),
+            dma((PHASES, ROWS)),
             dma((COLS,)),
-            dma((ITERS, COLS)),
+            dma((PHASES, COLS)),
         ],
         compiler_params=pltpu.CompilerParams(
             collective_id=0, has_side_effects=True, vmem_limit_bytes=58 * MIB
@@ -587,11 +643,12 @@
     found, windows, fs, fa, weight = tables()
     t = jnp.stack([tmatrix[:, :BLK], tmatrix[:, BLK:]])
     t = jnp.pad(t, ((0, 0), (0, LANES - BLK), (0, HALF - BLK)))
-    pad = jnp.pad(panel.reshape(2, BLK, 128), ((0, 0), (0, HALF - BLK), (0, 0)))
+    pad = panel.reshape(2, BLK, 2, 64).transpose(2, 1, 0, 3).reshape(2, BLK, 128)
+    pad = jnp.pad(pad, ((0, 0), (0, HALF - BLK), (0, 0)))
     weight = jnp.asarray(np.pad(weight, (0, TPAD - NT)).reshape(1, TPAD))
     u = steps(
         t,
-        pad.reshape(2 * HALF, 128),
+        pad,
         contrast,
         weight,
         jnp.asarray(windows),
@@ -599,7 +656,7 @@
         jnp.asarray(fa),
         found,
     )
-    return jnp.concatenate([u[:BLK], u[HALF : HALF + BLK]], axis=0)
+    return u[:, :BLK].reshape(2, BLK, 2, 64).transpose(2, 1, 0, 3).reshape(2 * BLK, 128)
 
 
 def solution(mesh):

time: 166 us -> 176 us (1.060)
  Pallas kernels: 159 us -> 167 us
  local copies, waits for them, and re-layouts: 3.98 us -> 6.48 us
    pallas_call x1, Pallas kernels: 159 us -> 167 us  [steps(): pl.pallas_call(functools.partial(step_kernel, plan, found), out_shape=jax...]
    reshape x1 -> x4, local copies, waits for them, and re-layouts: 0.07 us -> 2.23 us  [the longest x2 1.56 us: body(): u[:, :BLK].reshape(2, BLK, 2, 64).transpose(2, 1, 0, 3)]
where the time goes in v1:
time: 176 us; the launch traced here: 175 us
  Pallas kernels  167 us (95%)
  local copies, waits for them, and re-layouts  6.48 us (4%)
    pallas_call x1, Pallas kernels, steps(): pl.pallas_call(functools.partial(step_kernel, plan, found), out_shape=jax...  167 us

profile of v1, /device:TPU:25, one launch (start us, length us, event | category | flops | bytes accessed | tf_op | source)
XLA Modules:
  0.0 174.8 jit_solution(18274112320667040206)
XLA Ops:
  0.0 2.1 %slice_bitcast_fusion.1 = (bf16[1,666,666]{2,1,0:T(8,128)(2,1)S(1)}, bf16[1,666,666]{2,1,0:T(8,128)(2,1)S(1)}) fusion(bf16[666,1332]{1,0:T(8,128)(2,1)} %param.7), kind=kLoop, calls=%fused_computation.9 | loop fusion | bytes 3548448 | tf_op jit(solution)/shard_map/stack | solution.py:644
  2.1 0.0 copy-start
  2.1 1.7 fusion.5.t_ref
  3.8 0.0 copy-done
  3.8 0.2 copy.10
  4.0 0.5 reshape.12
  4.5 0.2 copy.12
  4.7 0.8 pad.9.panel_ref
  5.5 166.6 %steps.1 = bf16[2,672,128]{2,1,0:T(8,128)(2,1)} custom-call(bf16[2,768,672]{2,1,0:T(8,128)(2,1)} %fusion.5.t_ref, bf16[2,672,128]{2,1,0:T(8,128)(2,1)} %pad.9.panel_ref, f32[3,144,288]{2,1,0:T(8,128)} %contrast_ref.1, f32[1,256]{1,0:T(1,128)} %constant.11.clone.weight_ref, bf16[188,128,256]{2,1,0:T(8,128)(2,1)} %constant.12.clone.w_hbm, ...), custom_call_target="tpu_custom_call" | custom-call | tf_op jit(solution)/shard_map/steps/pallas_call | solution.py:603
  172.1 1.1 copy.13
  173.3 0.5 copy.16
  173.8 1.1 reshape.16
  (1 shorter events, 0.0 us)
Async XLA Ops:
  2.1 1.7 copy-start

commit v2 on v0

--- a/solution.py
+++ b/solution.py
@@ -25,6 +25,7 @@
 LANES = 768
 WIN = LANES // 128
 TPAD = 256
+KPAD = 1408
 QPAD = 160
 PER = 16
 MIB = 1024 * 1024
@@ -156,7 +157,7 @@
         analysis(PER + k, cw_ref[1] * first + cw_ref[2] * second)
         return carry
 
-    lax.fori_loop(0, PER, column, 0, unroll=2)
+    lax.fori_loop(0, PER, column, 0, unroll=4)
 
 
 def legendre_out(found, w_ref, spec, b_ref, done):
@@ -305,6 +306,7 @@
     s_in,
     b_out,
     b_in,
+    t_pad,
     w_ref,
     cw_ref,
     lat,
@@ -332,7 +334,9 @@
 
     table_copy = pltpu.make_async_copy(w_hbm, w_ref, w_sem)
     table_copy.start()
-    held[0, row] = panel_ref[...]
+    for first in range(ITERS):
+        held[first, row, 2 * HALF - 16 :] = jnp.zeros((16, 128), bf16)
+    held[0, row, : 2 * BLK] = panel_ref[...]
     greet(
         [{"row": (row + k) % ROWS} for k in range(1, ROWS)]
         + [{"col": (col + k) % COLS} for k in range(1, COLS)]
@@ -425,9 +429,7 @@
         here = s % 4
         for chunk in range(LANES // 256):
             rows = slice(chunk * 256, (chunk + 1) * 256)
-            value = dot(t_ref[0, rows], held[it, block, 0:HALF])
-            value += dot(t_ref[1, rows], held[it, block, HALF : 2 * HALF])
-            prod[here, :, rows] = value.T
+            prod[here, :, rows] = dot(t_pad[rows, : 2 * HALF], held[it, block]).T
         start = pl.multiple_of((1 - core) * 64, 64)
         mate_out[s] = prod[here, pl.ds(start, 64), :].astype(bf16)
         mate_copy(it, s).start()
@@ -455,6 +457,11 @@
             turned = contrast_ref[part].T * weight_ref[:, :NT]
             cw_ref[part] = jnp.concatenate([turned, jnp.zeros((NP, TPAD - NT), f32)], axis=1)
         lat[:, NQ * 32 :, :] = jnp.zeros((2, QPAD * 32 - NQ * 32, 128), f32)
+
+    def pad_t():
+        t_pad[656:, :] = jnp.zeros((LANES - 656, KPAD), bf16)
+        t_pad[:, KPAD - 128 :] = jnp.zeros((LANES, 128), bf16)
+        t_pad[:BLK, : 2 * BLK] = t_ref[...]
 
     def iteration(it, carry):
         s = 0
@@ -467,6 +474,8 @@
                 there = ((rel[0] + STEP[way][0]) % NX, (rel[1] + STEP[way][1]) % NZ)
                 ring_copy(it, part, rel, way, slot[(part, there, way)]).wait_recv()
             else:
+                if s == 0:
+                    pl.when(it == 0)(pad_t)
                 multiply(it, s, event[1])
                 if s == 0:
                     pl.when(it == 0)(prepare)
@@ -475,10 +484,11 @@
                 if s >= 7:
                     add_y(it, s - 7)
                 s += 1
-        for late in range(ROWS, ROWS + 3):
-            add_mate(it, late - 3)
-            add_y(it, late - 7)
-        for late in range(ROWS - 4, ROWS):
+        add_mate(it, ROWS - 3)
+        add_mate(it, ROWS - 2)
+        add_y(it, ROWS - 7)
+        add_mate(it, ROWS - 1)
+        for late in range(ROWS - 6, ROWS):
             add_y(it, late)
         pl.when(it == 0)(table_copy.wait)
         for s in range(1, ROWS):
@@ -514,18 +524,19 @@
             def _():
                 b_arrival(it, k).wait_recv()
 
+        parts = []
         for half in range(2):
-            rows = slice(half * HALF, (half + 1) * HALF)
             value = jnp.concatenate([b_in[it, k, half].astype(f32) for k in range(COLS)], axis=0)
-            value = (value.T[:HALF] + panel_ref[rows].astype(f32)).astype(bf16)
-
-            @pl.when(it == 0)
-            def _():
-                held[1, row, rows] = value
-
-            @pl.when(it == 1)
-            def _():
-                out_ref[rows] = value
+            parts.append(value.T[:BLK])
+        value = (jnp.concatenate(parts, axis=0) + panel_ref[...].astype(f32)).astype(bf16)
+
+        @pl.when(it == 0)
+        def _():
+            held[1, row, : 2 * BLK] = value
+
+        @pl.when(it == 1)
+        def _():
+            out_ref[...] = value
 
         for k in range(COLS):
 
@@ -546,7 +557,7 @@
     bf16, f32 = jnp.bfloat16, jnp.float32
     return pl.pallas_call(
         functools.partial(step_kernel, plan, found),
-        out_shape=jax.ShapeDtypeStruct((2 * HALF, 128), bf16),
+        out_shape=jax.ShapeDtypeStruct((2 * BLK, 128), bf16),
         in_specs=[vmem] * 4 + [pl.BlockSpec(memory_space=pl.ANY)] + [vmem] * 2,
         out_specs=vmem,
         scratch_shapes=[
@@ -560,6 +571,7 @@
             pltpu.VMEM((ITERS, ROWS, PER, LANES), bf16),
             pltpu.VMEM((ROWS, PER, LANES), bf16),
             pltpu.VMEM((ITERS, COLS, 2, PER, LANES), bf16),
+            pltpu.VMEM((LANES, KPAD), bf16),
             pltpu.VMEM(w.shape, bf16),
             pltpu.VMEM((3, NP, TPAD), f32),
             pltpu.VMEM((2, QPAD * 32, 128), f32),
@@ -585,13 +597,10 @@
 
 def body(tmatrix, panel, contrast):
     found, windows, fs, fa, weight = tables()
-    t = jnp.stack([tmatrix[:, :BLK], tmatrix[:, BLK:]])
-    t = jnp.pad(t, ((0, 0), (0, LANES - BLK), (0, HALF - BLK)))
-    pad = jnp.pad(panel.reshape(2, BLK, 128), ((0, 0), (0, HALF - BLK), (0, 0)))
     weight = jnp.asarray(np.pad(weight, (0, TPAD - NT)).reshape(1, TPAD))
-    u = steps(
-        t,
-        pad.reshape(2 * HALF, 128),
+    return steps(
+        tmatrix,
+        panel,
         contrast,
         weight,
         jnp.asarray(windows),
@@ -599,7 +608,6 @@
         jnp.asarray(fa),
         found,
     )
-    return jnp.concatenate([u[:BLK], u[HALF : HALF + BLK]], axis=0)
 
 
 def solution(mesh):

time: 166 us -> 158 us (0.952)
  Pallas kernels: 159 us -> 156 us
  other arithmetic: 2.46 us -> 0 us
  local copies, waits for them, and re-layouts: 3.98 us -> 1.73 us
    pallas_call x1, Pallas kernels: 159 us -> 156 us  [steps(): pl.pallas_call(functools.partial(step_kernel, plan, found), out_shape=jax...]
    another operation x1 -> x0, local copies, waits for them, and re-layouts: 2.12 us -> none  [body(): t = jnp.stack([tmatrix[:, :BLK], tmatrix[:, BLK:]])]
    unnamed x2 -> x1, local copies, waits for them, and re-layouts: 0.01 us -> 1.73 us
    another operation x1 -> x0, other arithmetic: 1.67 us -> none  [body(): t = jnp.stack([tmatrix[:, :BLK], tmatrix[:, BLK:]])]
where the time goes in v2:
time: 158 us
  Pallas kernels  156 us (99%)
  local copies, waits for them, and re-layouts  1.73 us (1%)
    pallas_call x1, Pallas kernels, steps(): pl.pallas_call(functools.partial(step_kernel, plan, found), out_shape=jax...  156 us

profile of v2, /device:TPU:25, one launch (start us, length us, event | category | flops | bytes accessed | tf_op | source)
XLA Modules:
  0.0 158.2 jit_solution(1857245434844549194)
XLA Ops:
  0.0 156.5 %steps.1 = bf16[1332,128]{1,0:T(8,128)(2,1)} custom-call(bf16[666,1332]{1,0:T(8,128)(2,1)} %t_ref.1, bf16[1332,128]{1,0:T(8,128)(2,1)} %panel_ref.1, f32[3,144,288]{2,1,0:T(8,128)} %contrast_ref.1, f32[1,256]{1,0:T(1,128)} %constant.8.clone.weight_ref, bf16[188,128,256]{2,1,0:T(8,128)(2,1)} %constant.9.clone.w_hbm, ...), custom_call_target="tpu_custom_call" | custom-call | tf_op jit(solution)/shard_map/steps/pallas_call | solution.py:558
  156.5 1.7 %copy.9 = bf16[1332,128]{1,0:T(8,128)(2,1)} copy(bf16[1332,128]{1,0:T(8,128)(2,1)} %steps.1) | data formatting | bytes 681984

commit v3 on v2

--- a/solution.py
+++ b/solution.py
@@ -27,6 +27,8 @@
 TPAD = 256
 KPAD = 1408
 QPAD = 160
+QH = QPAD // 2
+PH = 160
 PER = 16
 MIB = 1024 * 1024
 MESH = pl.DeviceIdType.MESH
@@ -105,13 +107,23 @@
     for index, (block, window, q, rows) in enumerate(found):
         for place, level in rows:
             windows[index, place, :NT] = legendre[q, level]
-    padded = np.zeros((QPAD, NP))
-    padded[:NQ] = fourier
+    parts = np.zeros((2, QH, PH))
+    parts[0, : LDEG + 1, : NP // 2 + 1] = fourier[: LDEG + 1, : NP // 2 + 1]
+    parts[1, :LDEG, : NP // 2 + 1] = fourier[LDEG + 1 :, : NP // 2 + 1]
+    high, low = split(parts)
+    synthesis = np.concatenate([high, low, high], axis=1).transpose(0, 2, 1)
+    analysis = np.concatenate([high, low], axis=1)
+    mirror = np.zeros((2, PH, NP), np.float32)
+    for p in range(NP // 2 + 1):
+        mirror[0, p, p] = 1.0
+        if 0 < p < NP // 2:
+            mirror[1, p, NP - p] = 1.0
     return (
         [f[:3] for f in found],
         windows.astype(np.float32).astype(ml_dtypes.bfloat16),
-        split(np.ascontiguousarray(padded.T)),
-        split(padded),
+        np.ascontiguousarray(synthesis),
+        analysis,
+        mirror.astype(ml_dtypes.bfloat16),
         weight.astype(np.float32),
     )
 
@@ -123,6 +135,10 @@
 def two(value):
     high = value.astype(jnp.bfloat16)
     return high, (value - high.astype(jnp.float32)).astype(jnp.bfloat16)
+
+
+def row_of(q):
+    return 32 * (q if q <= LDEG else q - LDEG - 1 + QH)
 
 
 def legendre_in(found, coefficients, w_ref, lat):
@@ -135,26 +151,34 @@
             term = dot(coefficients(block, window), w_ref[index])
             total = term if total is None else total + term
         for half in range(2):
-            lat[half, q * 32 : (q + 1) * 32, :] = total[:, half * 128 : half * 128 + 128]
+            lat[half, row_of(q) : row_of(q) + 32, :] = total[:, half * 128 : half * 128 + 128]
 
 
 def columns(fs_ref, fa_ref, cw_ref, lat, spec):
     def synthesis(place):
         rows = pl.ds(place, QPAD, stride=32)
         high, low = two(jnp.concatenate([lat[0, rows, :], lat[1, rows, :]], axis=1))
-        return dot(fs_ref[0], high) + dot(fs_ref[1], high) + dot(fs_ref[0], low)
-
-    def analysis(place, value):
-        high, low = two(value)
-        value = dot(fa_ref[0], high) + dot(fa_ref[1], high) + dot(fa_ref[0], low)
+        even, odd = [
+            dot(fs_ref[k], jnp.concatenate([high[part], high[part], low[part]], axis=0))
+            for k, part in enumerate((slice(0, QH), slice(QH, QPAD)))
+        ]
+        return even + odd, even - odd
+
+    def analysis(place, values):
+        found = []
+        for k, value in enumerate((values[0] + values[1], values[0] - values[1])):
+            high, low = two(value)
+            both = dot(fa_ref[k], high)
+            found.append(both[:QH] + both[QH:] + dot(fa_ref[k, :QH], low))
+        value = jnp.concatenate(found, axis=0)
         for half in range(2):
             spec[half, pl.ds(place, QPAD, stride=32), :] = value[:, half * 128 : half * 128 + 128]
 
     def column(k, carry):
         first = synthesis(k)
         second = synthesis(PER + k)
-        analysis(k, cw_ref[0] * first + cw_ref[1] * second)
-        analysis(PER + k, cw_ref[1] * first + cw_ref[2] * second)
+        analysis(k, [cw_ref[i, 0] * first[i] + cw_ref[i, 1] * second[i] for i in range(2)])
+        analysis(PER + k, [cw_ref[i, 1] * first[i] + cw_ref[i, 2] * second[i] for i in range(2)])
         return carry
 
     lax.fori_loop(0, PER, column, 0, unroll=4)
@@ -167,7 +191,7 @@
     for (block, window), members in sorted(by_window.items()):
         total = None
         for index, q in members:
-            rows = slice(q * 32, (q + 1) * 32)
+            rows = slice(row_of(q), row_of(q) + 32)
             high, low = two(jnp.concatenate([spec[0, rows, :], spec[1, rows, :]], axis=1))
             term = lax.dot_general(
                 jnp.concatenate([high, low], axis=0),
@@ -295,6 +319,7 @@
     w_hbm,
     fs_ref,
     fa_ref,
+    mirror_ref,
     out_ref,
     held,
     prod,
@@ -455,8 +480,20 @@
     def prepare():
         for part in range(3):
             turned = contrast_ref[part].T * weight_ref[:, :NT]
-            cw_ref[part] = jnp.concatenate([turned, jnp.zeros((NP, TPAD - NT), f32)], axis=1)
-        lat[:, NQ * 32 :, :] = jnp.zeros((2, QPAD * 32 - NQ * 32, 128), f32)
+            turned = jnp.concatenate([turned, jnp.zeros((NP, TPAD - NT), f32)], axis=1)
+            high, rest = turned.astype(bf16), turned
+            pieces = []
+            for _ in range(3):
+                pieces.append(high)
+                rest = rest - high.astype(f32)
+                high = rest.astype(bf16)
+            for side in range(2):
+                picked = [dot(mirror_ref[side], piece) for piece in pieces]
+                cw_ref[side, part] = picked[0] + picked[1] + picked[2]
+        for first in (LDEG + 1, QH + LDEG):
+            lat[:, first * 32 : (QH if first < QH else QPAD) * 32, :] = jnp.zeros(
+                (2, ((QH if first < QH else QPAD) - first) * 32, 128), f32
+            )
 
     def pad_t():
         t_pad[656:, :] = jnp.zeros((LANES - 656, KPAD), bf16)
@@ -549,7 +586,7 @@
     lax.fori_loop(0, ITERS, iteration, 0)
 
 
-def steps(t, panel, contrast, weight, w, fs, fa, found):
+def steps(t, panel, contrast, weight, w, fs, fa, mirror, found):
     plan = ring_plan()
     sends = sum(event[0] == "send" for event in plan)
     vmem = pl.BlockSpec(memory_space=pltpu.VMEM)
@@ -558,7 +595,7 @@
     return pl.pallas_call(
         functools.partial(step_kernel, plan, found),
         out_shape=jax.ShapeDtypeStruct((2 * BLK, 128), bf16),
-        in_specs=[vmem] * 4 + [pl.BlockSpec(memory_space=pl.ANY)] + [vmem] * 2,
+        in_specs=[vmem] * 4 + [pl.BlockSpec(memory_space=pl.ANY)] + [vmem] * 3,
         out_specs=vmem,
         scratch_shapes=[
             pltpu.VMEM((ITERS, ROWS, 2 * HALF, 128), bf16),
@@ -573,7 +610,7 @@
             pltpu.VMEM((ITERS, COLS, 2, PER, LANES), bf16),
             pltpu.VMEM((LANES, KPAD), bf16),
             pltpu.VMEM(w.shape, bf16),
-            pltpu.VMEM((3, NP, TPAD), f32),
+            pltpu.VMEM((2, 3, PH, TPAD), f32),
             pltpu.VMEM((2, QPAD * 32, 128), f32),
             pltpu.VMEM((2, QPAD * 32, 128), f32),
             dma(()),
@@ -592,11 +629,11 @@
             collective_id=0, has_side_effects=True, vmem_limit_bytes=58 * MIB
         ),
         name="steps",
-    )(t, panel, contrast, weight, w, fs, fa)
+    )(t, panel, contrast, weight, w, fs, fa, mirror)
 
 
 def body(tmatrix, panel, contrast):
-    found, windows, fs, fa, weight = tables()
+    found, windows, fs, fa, mirror, weight = tables()
     weight = jnp.asarray(np.pad(weight, (0, TPAD - NT)).reshape(1, TPAD))
     return steps(
         tmatrix,
@@ -606,6 +643,7 @@
         jnp.asarray(windows),
         jnp.asarray(fs),
         jnp.asarray(fa),
+        jnp.asarray(mirror),
         found,
     )
 

time: 158 us -> 160 us (1.013)
  Pallas kernels: 156 us -> 158 us
    pallas_call x1, Pallas kernels: 156 us -> 158 us  [steps(): pl.pallas_call(functools.partial(step_kernel, plan, found), out_shape=jax...]
where the time goes in v3:
time: 160 us
  Pallas kernels  158 us (99%)
  local copies, waits for them, and re-layouts  1.73 us (1%)
    pallas_call x1, Pallas kernels, steps(): pl.pallas_call(functools.partial(step_kernel, plan, found), out_shape=jax...  158 us

profile of v3, /device:TPU:25, one launch (start us, length us, event | category | flops | bytes accessed | tf_op | source)
XLA Modules:
  0.0 160.0 jit_solution(18075287701997438211)
XLA Ops:
  0.0 158.3 %steps.1 = bf16[1332,128]{1,0:T(8,128)(2,1)} custom-call(bf16[666,1332]{1,0:T(8,128)(2,1)} %t_ref.1, bf16[1332,128]{1,0:T(8,128)(2,1)} %panel_ref.1, f32[3,144,288]{2,1,0:T(8,128)} %contrast_ref.1, f32[1,256]{1,0:T(1,128)} %constant.10.clone.weight_ref, bf16[188,128,256]{2,1,0:T(8,128)(2,1)} %constant.11.clone.w_hbm, ...), custom_call_target="tpu_custom_call" | custom-call | tf_op jit(solution)/shard_map/steps/pallas_call | solution.py:595
  158.3 1.7 %copy.10 = bf16[1332,128]{1,0:T(8,128)(2,1)} copy(bf16[1332,128]{1,0:T(8,128)(2,1)} %steps.1) | data formatting | bytes 681984

commit v4 on v3

--- a/solution.py
+++ b/solution.py
@@ -28,6 +28,7 @@
 KPAD = 1408
 QPAD = 160
 QH = QPAD // 2
+CS = 40
 PH = 160
 PER = 16
 MIB = 1024 * 1024
@@ -138,7 +139,7 @@
 
 
 def row_of(q):
-    return 32 * (q if q <= LDEG else q - LDEG - 1 + QH)
+    return CS * (q if q <= LDEG else q - LDEG - 1 + QH)
 
 
 def legendre_in(found, coefficients, w_ref, lat):
@@ -156,7 +157,7 @@
 
 def columns(fs_ref, fa_ref, cw_ref, lat, spec):
     def synthesis(place):
-        rows = pl.ds(place, QPAD, stride=32)
+        rows = pl.ds(place, QPAD, stride=CS)
         high, low = two(jnp.concatenate([lat[0, rows, :], lat[1, rows, :]], axis=1))
         even, odd = [
             dot(fs_ref[k], jnp.concatenate([high[part], high[part], low[part]], axis=0))
@@ -172,7 +173,7 @@
             found.append(both[:QH] + both[QH:] + dot(fa_ref[k, :QH], low))
         value = jnp.concatenate(found, axis=0)
         for half in range(2):
-            spec[half, pl.ds(place, QPAD, stride=32), :] = value[:, half * 128 : half * 128 + 128]
+            spec[half, pl.ds(place, QPAD, stride=CS), :] = value[:, half * 128 : half * 128 + 128]
 
     def column(k, carry):
         first = synthesis(k)
@@ -491,8 +492,8 @@
                 picked = [dot(mirror_ref[side], piece) for piece in pieces]
                 cw_ref[side, part] = picked[0] + picked[1] + picked[2]
         for first in (LDEG + 1, QH + LDEG):
-            lat[:, first * 32 : (QH if first < QH else QPAD) * 32, :] = jnp.zeros(
-                (2, ((QH if first < QH else QPAD) - first) * 32, 128), f32
+            lat[:, first * CS : (QH if first < QH else QPAD) * CS, :] = jnp.zeros(
+                (2, ((QH if first < QH else QPAD) - first) * CS, 128), f32
             )
 
     def pad_t():
@@ -611,8 +612,8 @@
             pltpu.VMEM((LANES, KPAD), bf16),
             pltpu.VMEM(w.shape, bf16),
             pltpu.VMEM((2, 3, PH, TPAD), f32),
-            pltpu.VMEM((2, QPAD * 32, 128), f32),
-            pltpu.VMEM((2, QPAD * 32, 128), f32),
+            pltpu.VMEM((2, QPAD * CS, 128), f32),
+            pltpu.VMEM((2, QPAD * CS, 128), f32),
             dma(()),
             dma((sends,)),
             dma((ITERS, sends)),

time: 160 us -> 144 us (0.900)
  Pallas kernels: 158 us -> 142 us
    pallas_call x1, Pallas kernels: 158 us -> 142 us  [steps(): pl.pallas_call(functools.partial(step_kernel, plan, found), out_shape=jax...]
where the time goes in v4:
time: 144 us
  Pallas kernels  142 us (99%)
  local copies, waits for them, and re-layouts  1.73 us (1%)
    pallas_call x1, Pallas kernels, steps(): pl.pallas_call(functools.partial(step_kernel, plan, found), out_shape=jax...  142 us

profile of v4, /device:TPU:25, one launch (start us, length us, event | category | flops | bytes accessed | tf_op | source)
XLA Modules:
  0.0 144.2 jit_solution(1274602036750652219)
XLA Ops:
  0.0 142.5 %steps.1 = bf16[1332,128]{1,0:T(8,128)(2,1)} custom-call(bf16[666,1332]{1,0:T(8,128)(2,1)} %t_ref.1, bf16[1332,128]{1,0:T(8,128)(2,1)} %panel_ref.1, f32[3,144,288]{2,1,0:T(8,128)} %contrast_ref.1, f32[1,256]{1,0:T(1,128)} %constant.10.clone.weight_ref, bf16[188,128,256]{2,1,0:T(8,128)(2,1)} %constant.11.clone.w_hbm, ...), custom_call_target="tpu_custom_call" | custom-call | tf_op jit(solution)/shard_map/steps/pallas_call | solution.py:596
  142.5 1.7 %copy.10 = bf16[1332,128]{1,0:T(8,128)(2,1)} copy(bf16[1332,128]{1,0:T(8,128)(2,1)} %steps.1) | data formatting | bytes 681984

commit v5 on v4

--- a/solution.py
+++ b/solution.py
@@ -182,7 +182,7 @@
         analysis(PER + k, [cw_ref[i, 1] * first[i] + cw_ref[i, 2] * second[i] for i in range(2)])
         return carry
 
-    lax.fori_loop(0, PER, column, 0, unroll=4)
+    lax.fori_loop(0, PER, column, 0, unroll=8)
 
 
 def legendre_out(found, w_ref, spec, b_ref, done):

time: 144 us -> 143 us (level)
  no operation moved by 1% of the time
where the time goes in v5:
time: 143 us
  Pallas kernels  142 us (99%)
  local copies, waits for them, and re-layouts  1.73 us (1%)
    pallas_call x1, Pallas kernels, steps(): pl.pallas_call(functools.partial(step_kernel, plan, found), out_shape=jax...  142 us

profile of v5, /device:TPU:25, one launch (start us, length us, event | category | flops | bytes accessed | tf_op | source)
XLA Modules:
  0.0 143.3 jit_solution(13579610962672572887)
XLA Ops:
  0.0 141.5 %steps.1 = bf16[1332,128]{1,0:T(8,128)(2,1)} custom-call(bf16[666,1332]{1,0:T(8,128)(2,1)} %t_ref.1, bf16[1332,128]{1,0:T(8,128)(2,1)} %panel_ref.1, f32[3,144,288]{2,1,0:T(8,128)} %contrast_ref.1, f32[1,256]{1,0:T(1,128)} %constant.10.clone.weight_ref, bf16[188,128,256]{2,1,0:T(8,128)(2,1)} %constant.11.clone.w_hbm, ...), custom_call_target="tpu_custom_call" | custom-call | tf_op jit(solution)/shard_map/steps/pallas_call | solution.py:596
  141.5 1.7 %copy.10 = bf16[1332,128]{1,0:T(8,128)(2,1)} copy(bf16[1332,128]{1,0:T(8,128)(2,1)} %steps.1) | data formatting | bytes 681984
